TPU v7x, 1024 devices: a whole 8x8x8 slice. The times are simulated.
1024 devices in a mesh: dp: 16 (over z, x_hi), ctx: 8 (over y), tp: 8 (over x_lo, core).
Axes of the slice: x: 8 (x_hi: 2, x_lo: 4; x = x_hi * 4 + x_lo), y: 8, z: 8, core: 2. Of those that a mesh axis runs over, the one named last changes fastest.
Arguments:
- tokens: bfloat16 [8192, 3072], P(('dp', 'ctx'), 'tp'), may hold values from -6 to 6
- expert_ids: int32 [8192, 2], P(('dp', 'ctx')), may hold values from 0 to 7, all different within a row; in each aligned block of 64 rows (0 to 63, 64 to 127, ...) at most 18 rows name the same one
- weights: bfloat16 [8, 3072, 8192], P('ctx', None, 'tp'), may hold values from -0.109375 to 0.109375
- cotangent: bfloat16 [16, 8, 144, 8192], P('dp', 'ctx', None, 'tp'), may hold values from -6 to 6
Outputs:
- hidden: bfloat16 [16, 8, 144, 8192], P('dp', 'ctx', None, 'tp')
- weight_grad: bfloat16 [8, 3072, 8192], P('ctx', 'dp', 'tp')
- token_grad: bfloat16 [8192, 3072], P(('dp', 'ctx'), 'tp')
Inputs may be any that keep to these rules, and one draw needn't show every extreme that they name: `expert_ids`: the two experts of a token differ. Among the tokens of one aligned block of 64 tokens no expert is named more than 18 times, and in some block one expert is named exactly 18 times.
All inputs are finite; a program needn't handle non-finite values.
Results may differ from a plain program's by a relative error of at most 0.02.
Values may be sent and summed in bfloat16 or wider, within the bound.
A program may use at most 64 MiB of HBM per device.

v0:
```python
import jax
import jax.numpy as jnp
from jax import lax
from jax.sharding import PartitionSpec as P


def slot_chooser(expert_ids, experts, capacity):
    routed = expert_ids.reshape(-1)
    onehot = (routed[:, None] == jnp.arange(experts, dtype=jnp.int32)[None, :]).astype(jnp.int32)
    before = jnp.cumsum(onehot, axis=0) - onehot
    target = routed * capacity + jnp.sum(before * onehot, axis=1)
    places = jnp.arange(experts * capacity, dtype=jnp.int32)
    return (places[:, None] == target[None, :]).astype(jnp.bfloat16)


def per_device(tokens, expert_ids, weights, cotangent):
    experts = lax.axis_size("ctx")
    slot_count = cotangent.shape[2]
    capacity = slot_count // experts
    chooser = slot_chooser(expert_ids, experts, capacity)
    wide = lax.all_gather(tokens, "tp", axis=1, tiled=True)
    route_rows = jnp.repeat(wide, 2, axis=0)
    buffer = jnp.dot(chooser, route_rows, preferred_element_type=jnp.float32).astype(jnp.bfloat16)
    buffer = buffer.reshape(experts, capacity, wide.shape[1])
    received = lax.all_to_all(buffer, "ctx", split_axis=0, concat_axis=0, tiled=True)
    rows = received.reshape(slot_count, wide.shape[1])
    weight_local = weights[0]
    preact = jnp.dot(rows, weight_local, preferred_element_type=jnp.float32)
    gate_sig = jax.nn.sigmoid(preact)
    hidden = (preact * gate_sig).astype(jnp.bfloat16)
    slope = (
        cotangent[0, 0].astype(jnp.float32) * gate_sig * (1.0 + preact * (1.0 - gate_sig))
    ).astype(jnp.bfloat16)
    partial_back = lax.dot_general(
        slope, weight_local, (((1,), (1,)), ((), ())), preferred_element_type=jnp.float32
    )
    summed = lax.psum_scatter(
        partial_back.astype(jnp.bfloat16), "tp", scatter_dimension=1, tiled=True
    ).astype(jnp.float32)
    summed = summed.astype(jnp.bfloat16).reshape(experts, capacity, summed.shape[1])
    home = lax.all_to_all(summed, "ctx", split_axis=0, concat_axis=0, tiled=True)
    home_flat = home.reshape(experts * capacity, home.shape[2])
    picked = lax.dot_general(
        chooser, home_flat, (((0,), (0,)), ((), ())), preferred_element_type=jnp.float32
    )
    token_grad = picked.reshape(tokens.shape[0], 2, home.shape[2]).sum(axis=1).astype(jnp.bfloat16)
    grad_share = lax.psum_scatter(
        lax.dot_general(
            rows, slope, (((0,), (0,)), ((), ())), preferred_element_type=jnp.float32
        ).astype(jnp.bfloat16),
        "dp",
        scatter_dimension=0,
        tiled=True,
    )
    weight_grad = grad_share[None]
    return (hidden[None, None], weight_grad, token_grad)


def solution(mesh):
    placed = (
        P(("dp", "ctx"), "tp"),
        P(("dp", "ctx"), None),
        P("ctx", None, "tp"),
        P("dp", "ctx", None, "tp"),
    )
    return jax.shard_map(
        per_device,
        mesh=mesh,
        in_specs=placed,
        out_specs=(P("dp", "ctx", None, "tp"), P("ctx", "dp", "tp"), P(("dp", "ctx"), "tp")),
        check_vma=False,
    )
```

profile of v0, /device:TPU:1, one launch (start us, length us, event | category | flops | bytes accessed | tf_op | source)
XLA Modules:
  0.0 400.0 jit_solution(14270943131808028597)
XLA Ops:
  7.2 0.0 reduce-scatter.7.cloned.1.call-start
  7.2 0.8 copy.10
  8.0 0.1 reshape.61
  8.1 0.1 fusion.11
  8.2 0.2 reduce_window_sum.11
  8.4 0.2 select_reduce_fusion
  8.6 28.8 %all_gather.3 = bf16[64,3072]{1,0:T(8,128)(2,1)S(1)} all-gather(bf16[64,384]{1,0:T(8,128)(2,1)} %param.4), channel_id=1, replica_groups=mesh['dp'=16,'ctx'=8,'tp'=8] {'tp'}, dimensions={1}, use_global_device_ids=true | all-gather | bytes 442368 | tf_op jit(solution)/shard_map/all_gather | solution.py:21
  37.3 0.4 broadcast_in_dim.12
  37.8 0.3 reshape.62
  38.1 0.4 convolution_convert_fusion.1
  38.4 0.3 reshape.63
  38.7 0.0 slice-start
  38.7 35.3 %all_to_all.10 = bf16[8,18,3072]{2,1,0:T(8,128)(2,1)} all-to-all(bf16[8,18,3072]{2,1,0:T(8,128)(2,1)S(1)} %reshape.63), channel_id=1, replica_groups=mesh['dp'=16,'ctx'=8,'tp'=8] {'ctx'}, dimensions={0} | all-to-all | bytes 1769472 | tf_op jit(solution)/shard_map/all_to_all | solution.py:25
  74.0 1.6 reshape.64
  75.6 0.0 slice-start.1
  75.6 4.9 %fusion.2 = f32[144,1024]{1,0:T(8,128)} fusion(bf16[144,3072]{1,0:T(8,128)(2,1)S(1)} %reshape.64, bf16[1,3072,1024]{2,1,0:T(8,128)(2,1)} %param.6), kind=kOutput, calls=%fused_computation.2 | convolution fusion | flops 905969664 | bytes 7766016 | tf_op jit(solution)/shard_map/dot_general | solution.py:28
  80.5 4.2 %fusion.4 = bf16[144,3072]{1,0:T(8,128)(2,1)} fusion(bf16[1,3072,1024]{2,1,0:T(8,128)(2,1)S(1)} %bitcast.23, f32[144,1024]{1,0:T(8,128)} %fusion.2, bf16[1,1,144,1024]{3,2,1,0:T(8,128)(2,1)S(1)} %copy-done), kind=kOutput, calls=%fused_computation.5 | convolution fusion | flops 907886592 | bytes 8060928 | tf_op jit(solution)/shard_map/dot_general | solution.py:34
  84.7 2.4 copy.12
  87.2 0.0 reduce-scatter.7.cloned.1.call-update
  87.2 0.0 reduce-scatter.5.cloned.1.call-start
  87.3 5.6 %convolution_convert_fusion = bf16[3072,1024]{1,0:T(8,128)(2,1)} fusion(bf16[144,3072]{1,0:T(8,128)(2,1)S(1)} %reshape.64, f32[144,1024]{1,0:T(8,128)} %fusion.2, bf16[1,1,144,1024]{3,2,1,0:T(8,128)(2,1)S(1)} %copy-done), kind=kOutput, calls=%fused_computation.4 | convolution fusion | flops 910589952 | bytes 8060928 | tf_op jit(solution)/shard_map/dot_general | solution.py:48
  92.9 0.0 reduce-scatter.5.cloned.1.call-update
  92.9 0.1 iota_compare_fusion
  93.0 0.1 eq.50
  93.1 34.4 %reduce-scatter.7.cloned.1.call-done = bf16[384,144]{1,0:T(8,128)(2,1)} async-done(((bf16[3072,144]{1,0:T(8,128)(2,1)}), bf16[384,144]{1,0:T(8,128)(2,1)}) %reduce-scatter.7.cloned.1.call-update) | async-done | bytes 110608
  127.4 1.0 copy.13
  128.5 0.7 reshape.65
  129.2 4.4 %all-to-all-start.1 = ((bf16[8,18,384]{2,1,0:T(8,128)(2,1)}), bf16[8,18,384]{2,1,0:T(8,128)(2,1)S(1)}, u32[]{:S(2)}, u32[]{:S(2)}) async-start(bf16[8,18,384]{2,1,0:T(8,128)(2,1)} %reshape.65), calls=%async_computation.2 | async-start | bytes 294912 | tf_op jit(solution)/shard_map/all_to_all | solution.py:41
  133.6 1.9 fusion.9
  135.5 6.2 %all-to-all-done.1 = bf16[8,18,384]{2,1,0:T(8,128)(2,1)S(1)} async-done(((bf16[8,18,384]{2,1,0:T(8,128)(2,1)}), bf16[8,18,384]{2,1,0:T(8,128)(2,1)S(1)}, u32[]{:S(2)}, u32[]{:S(2)}) %all-to-all-start.1) | async-done | bytes 110624 | tf_op jit(solution)/shard_map/all_to_all | solution.py:41
  141.7 0.8 convolution_reduce_fusion
  142.5 250.6 %reduce-scatter.5.cloned.1.call-done = bf16[192,1024]{1,0:T(8,128)(2,1)} async-done(((bf16[3072,1024]{1,0:T(8,128)(2,1)}), bf16[192,1024]{1,0:T(8,128)(2,1)}) %reduce-scatter.5.cloned.1.call-update) | async-done | bytes 393232 | tf_op jit(solution)/shard_map/reduce_scatter | solution.py:47
  (7 shorter events, 0.1 us)
Async XLA Ops:
  7.2 120.3 %reduce-scatter.7.cloned.1.call-start = ((), (), s32[]{:S(2)}) async-start(), calls=%async_computation.5 | async-start | bytes 1769472
  38.7 41.8 %slice-start = ((s8[6291456]{0:T(1024)(128)(4,1)}), s8[2097152]{0:T(1024)(128)(4,1)S(1)}, s32[]{:S(2)}) async-start(s8[6291456]{0:T(1024)(128)(4,1)} %bitcast.22), calls=%async_computation.6 | async-start | bytes 4194304
  74.0 6.5 %copy-start = (bf16[1,1,144,1024]{3,2,1,0:T(8,128)(2,1)S(1)}, bf16[1,1,144,1024]{3,2,1,0:T(8,128)(2,1)}, u32[]{:S(2)}) copy-start(bf16[1,1,144,1024]{3,2,1,0:T(8,128)(2,1)} %param.7) | copy-start | bytes 884740
  75.6 4.9 %slice-start.1 = ((s8[6291456]{0:T(1024)(128)(4,1)}), s8[4194304]{0:T(1024)(128)(4,1)S(1)}, s32[]{:S(2)}) async-start(s8[6291456]{0:T(1024)(128)(4,1)} %bitcast.22), calls=%async_computation.7 | async-start | bytes 8388608
  87.2 305.9 %reduce-scatter.5.cloned.1.call-start = ((), (), s32[]{:S(2)}) async-start(), calls=%async_computation.4 | async-start | bytes 6684672 | tf_op jit(solution)/shard_map/reduce_scatter | solution.py:47
  129.2 12.5 %all-to-all-start.1 = ((bf16[8,18,384]{2,1,0:T(8,128)(2,1)}), bf16[8,18,384]{2,1,0:T(8,128)(2,1)S(1)}, u32[]{:S(2)}, u32[]{:S(2)}) async-start(bf16[8,18,384]{2,1,0:T(8,128)(2,1)} %reshape.65), calls=%async_computation.2 | async-start | bytes 294912 | tf_op jit(solution)/shard_map/all_to_all | solution.py:41
Sparse Core Ops, SparseCore 0:
  87.3 40.0 reduce-scatter.6
  133.9 259.1 reduce-scatter.4
where the time goes:
time: 404 us; the launch traced here: 400 us
  waiting for transfers between devices  291 us (72%)
  blocking collectives  64 us (16%)
  matrix products  15.9 us (4%)
  between operations  14.1 us (3%)
  local copies, waits for them, and re-layouts  7.76 us (2%)
  starting transfers between devices  4.5 us (1%)
    reduce_scatter x1, waiting for transfers between devices, per_device(): lax.psum_scatter(lax.dot_general(rows, slope, (((0,), (0,)), ((), ())), p...  251 us
    all_to_all x1, blocking collectives, per_device(): lax.all_to_all(buffer, 'ctx', split_axis=0, concat_axis=0, tiled=True)  35.3 us
    unnamed x3, waiting for transfers between devices  34.4 us
    all_gather x1, blocking collectives, per_device(): wide = lax.all_gather(tokens, 'tp', axis=1, tiled=True)  28.8 us
  transfers between devices with their start and end apart: 3, of which 3 were waited for; matrix products, arithmetic and copies ran while one was open for 3% of the time, Pallas kernels for 0%

commit v1 on v0

v1 whole, which is shorter than its diff:
```python
import functools

import jax
import jax.numpy as jnp
from jax import lax
from jax.experimental import pallas as pl
from jax.experimental.pallas import tpu as pltpu
from jax.sharding import PartitionSpec as P

MESH = pl.DeviceIdType.MESH
BF16 = jnp.bfloat16
F32 = jnp.float32
HI = 2
CORES = 2
PARTS = 4


def xor(a, bits):
    for bit in (1, 2, 4, 8):
        if bits & bit:
            a = a + bit - 2 * bit * ((a // bit) % 2)
    return a


def nt(a, b):
    return lax.dot_general(a, b, (((1,), (1,)), ((), ())), preferred_element_type=F32)


def tn(a, b):
    return lax.dot_general(a, b, (((0,), (0,)), ((), ())), preferred_element_type=F32)


def nn(a, b):
    return jnp.dot(a, b, preferred_element_type=F32)


def kernel(
    dims,
    tokens, place, place_t, pack, unpack, w_hbm, cot,
    hidden, wgrad, tgrad,
    w, ysend, yrecv, g, r, acc, s, psend, precv, qsend, t, hsend, hrecv, wsend, wkeep, wrecv,
    w_sem, y_ss, y_rs, gd_ss, gd_rs, gf_ss, gf_rs, r_ss, rf_ss, r_rs, s_ss, s_rs,
    p_ss, p_rs, t_ss, t_rs, h_ss, h_rs, x_ss, x_rs,
):
    n_z, n_ctx, n_lo = dims
    feat = tokens.shape[1]
    cols = cot.shape[1] // PARTS
    half = feat // HI
    dp, e, j = lax.axis_index("dp"), lax.axis_index("ctx"), lax.axis_index("tp")
    z, hi = dp // HI, dp % HI
    lo, core = j // CORES, j % CORES
    waits = []

    def copy(src, dst, ssem, rsem, to):
        return pltpu.make_async_remote_copy(
            src_ref=src, dst_ref=dst, send_sem=ssem, recv_sem=rsem,
            device_id=to, device_id_type=MESH,
        )

    def send(*args):
        made = copy(*args)
        made.start()
        waits.append(made)

    def on_y(d):
        return (dp, (e + d) % n_ctx, j)

    def on_z(k):
        return (k * HI + hi, e, j)

    def on_lo(o):
        return (dp, e, xor(lo, o) * CORES + core)

    other = (dp, e, lo * CORES + 1 - core)
    across = (z * HI + 1 - hi, e, j)

    w_copy = pltpu.make_async_copy(w_hbm, w, w_sem)
    w_copy.start()

    partners = [on_y(d) for d in range(1, n_ctx)]
    partners += [on_z((z + d) % n_z) for d in range(1, n_z)]
    partners += [on_lo(o) for o in range(1, n_lo)]
    partners += [other, across]
    barrier = pltpu.get_barrier_semaphore()
    for to in partners:
        pl.semaphore_signal(barrier, inc=1, device_id=to, device_id_type=MESH)

    ysend[...] = nn(place[...], tokens[...]).astype(BF16).reshape(ysend.shape)
    pl.semaphore_wait(barrier, len(partners))

    far = sorted(range(1, n_ctx), key=lambda d: -min(d, n_ctx - d))
    for d in far:
        send(ysend.at[(e + d) % n_ctx], yrecv.at[e], y_ss.at[d - 1], y_rs.at[d - 1], on_y(d))
    yrecv[e] = ysend[e]
    for d in far:
        copy(ysend.at[0], yrecv.at[(e - d + n_ctx) % n_ctx], y_ss.at[d - 1], y_rs.at[d - 1], on_y(d)).wait_recv()
    g[j] = nn(pack[...], yrecv[...].reshape(-1, feat)).astype(BF16)

    for o in range(1, n_lo):
        send(g.at[j], g.at[j], gd_ss.at[o], gd_rs.at[o], on_lo(o))
    send(g.at[j], g.at[j], gf_ss.at[0], gf_rs.at[0], other)

    def rows_copy(o):
        k = xor(lo, o) * CORES + core
        return k, copy(g.at[k], r.at[z], r_ss.at[o], r_rs.at[z], on_z(k))

    def rows_start(o):
        k, made = rows_copy(o)

        @pl.when(k != z)
        def _():
            made.start()

    def project(k, first=False):
        @pl.loop(0, PARTS)
        def _(q):
            at = pl.ds(pl.multiple_of(q * cols, cols), cols)
            term = nn(g[k], w[pl.ds(pl.multiple_of(k * feat, feat), feat), at])
            acc[q] = term if first else acc[q] + term

    rows_start(0)
    w_copy.wait()
    project(j, True)
    k = lo * CORES + 1 - core
    copy(g.at[j], g.at[k], gf_ss.at[0], gf_rs.at[0], other).wait_recv()
    project(k)
    for o in range(1, n_lo):
        k = xor(lo, o) * CORES + core
        copy(g.at[j], g.at[k], gd_ss.at[o], gd_rs.at[o], on_lo(o)).wait_recv()
        send(g.at[k], g.at[k], gf_ss.at[o], gf_rs.at[o], other)
        rows_start(o)
        project(k)
    for o in range(1, n_lo):
        k = xor(lo, o) * CORES + 1 - core
        copy(g.at[j], g.at[k], gf_ss.at[o], gf_rs.at[o], other).wait_recv()
        project(k)

    def reach(way, q):
        return n_z // 2 if q % 2 == way else n_z - 1 - n_z // 2

    def step_to(way):
        return on_z((z + 1) % n_z if way == 0 else (z + n_z - 1) % n_z)

    def own(q):
        for way in (0, 1):
            send(s.at[q, z], s.at[q, z], s_ss.at[way, q, 0], s_rs.at[way, q, 0], step_to(way))

    def step(q, d):
        for way in (0, 1):
            if d <= reach(way, q):
                src = (z - d + n_z) % n_z if way == 0 else (z + d) % n_z
                copy(s.at[q, z], s.at[q, src], s_ss.at[way, q, d - 1], s_rs.at[way, q, d - 1], step_to(way)).wait_recv()
                if d < reach(way, q):
                    send(s.at[q, src], s.at[q, src], s_ss.at[way, q, d], s_rs.at[way, q, d], step_to(way))

    for q in range(PARTS):
        at = slice(q * cols, (q + 1) * cols)
        p = acc[q]
        gate = jax.nn.sigmoid(p)
        hidden[:, at] = (p * gate).astype(BF16)
        s[q, z] = (cot[:, at].astype(F32) * gate * (1.0 + p * (1.0 - gate))).astype(BF16)
        if q < 2:
            own(q)

    def back(k):
        rows = pl.ds(pl.multiple_of(k * feat, feat), feat)
        total = nt(s[0, z], w[rows, 0:cols])
        for q in range(1, PARTS):
            total = total + nt(s[q, z], w[rows, q * cols:(q + 1) * cols])
        return total

    for m in range(n_lo):
        psend[m] = back(m * CORES + 1 - core).astype(BF16)
        send(psend.at[m], precv.at[m], p_ss.at[m], p_rs.at[m], other)

    for d in (1,):
        step(0, d), step(1, d)

    for m in range(n_lo):
        copy(psend.at[m], precv.at[m], p_ss.at[m], p_rs.at[m], other).wait_recv()
    for o in (*range(1, n_lo), 0):
        m = xor(lo, o)
        qsend[o] = (back(m * CORES + core) + precv[m].astype(F32)).astype(BF16)
        if o:
            send(qsend.at[o], t.at[o], t_ss.at[o], t_rs.at[o], on_lo(o))

    for d in range(2, n_z // 2):
        step(0, d), step(1, d)
        if d == 2:
            own(2), own(3)
    if n_z // 2 <= 2:
        own(2), own(3)

    r[z] = g[z]
    for d in range(1, n_z):
        src = (z + d) % n_z
        copy(g.at[0], r.at[src], rf_ss.at[d - 1], r_rs.at[src], other).wait_recv()

        @pl.when(core == z % CORES)
        def _():
            copy(r.at[src], r.at[src], rf_ss.at[d - 1], r_rs.at[src], other).start()

    step(0, n_z // 2), step(1, n_z // 2)
    step(2, 1), step(3, 1)

    def product(q):
        right = s[q].reshape(-1, cols)
        whole = tn(r[...].reshape(-1, feat), right)
        wkeep[q] = whole
        theirs = wkeep[q, pl.ds(pl.multiple_of((1 - hi) * half, half), half), :]
        wsend[q] = theirs.astype(BF16)
        send(wsend.at[q], wrecv.at[q], x_ss.at[q], x_rs.at[q], across)

    product(0)
    product(1)
    step(2, 2), step(3, 2)

    summed = qsend[0].astype(F32)
    for o in range(1, n_lo):
        copy(qsend.at[o], t.at[o], t_ss.at[o], t_rs.at[o], on_lo(o)).wait_recv()
        summed = summed + t[o].astype(F32)
    hsend[...] = nn(unpack[...], summed.astype(BF16)).astype(BF16).reshape(hsend.shape)
    for d in far:
        send(hsend.at[(e + d) % n_ctx], hrecv.at[e], h_ss.at[d - 1], h_rs.at[d - 1], on_y(d))
    hrecv[e] = hsend[e]

    for d in range(3, n_z // 2 + 1):
        step(2, d), step(3, d)
    product(2)
    product(3)

    for d in far:
        copy(hsend.at[0], hrecv.at[(e - d + n_ctx) % n_ctx], h_ss.at[d - 1], h_rs.at[d - 1], on_y(d)).wait_recv()
    tgrad[...] = nn(place_t[...], hrecv[...].reshape(-1, feat)).astype(BF16)

    for q in range(PARTS):
        copy(wsend.at[q], wrecv.at[q], x_ss.at[q], x_rs.at[q], across).wait_recv()
        mine = wkeep[q, pl.ds(pl.multiple_of(hi * half, half), half), :]
        wgrad[:, q * cols:(q + 1) * cols] = (mine + wrecv[q].astype(F32)).astype(BF16)

    for made in waits:
        made.wait_send()
    for o in range(n_lo):
        k, made = rows_copy(o)

        @pl.when(k != z)
        def _():
            made.wait_send()

    @pl.when(core == z % CORES)
    def _():
        for d in range(1, n_z):
            src = (z + d) % n_z
            copy(r.at[src], r.at[src], rf_ss.at[d - 1], r_rs.at[src], other).wait_send()


def per_device(tokens, expert_ids, weights, cotangent):
    n_ctx, n_tp, n_dp = lax.axis_size("ctx"), lax.axis_size("tp"), lax.axis_size("dp")
    n_z, n_lo = n_dp // HI, n_tp // CORES
    count, feat = tokens.shape
    slots, ff = cotangent.shape[2:]
    capacity = slots // n_ctx
    padded = -(-capacity // 16) * 16
    cols, half = ff // PARTS, feat // HI

    routed = expert_ids.reshape(-1)
    onehot = (routed[:, None] == jnp.arange(n_ctx, dtype=jnp.int32)[None, :]).astype(jnp.int32)
    before = jnp.cumsum(onehot, axis=0) - onehot
    target = (routed * padded + jnp.sum(before * onehot, axis=1)).reshape(count, 2)
    places = jnp.arange(n_ctx * padded, dtype=jnp.int32)
    place = ((places[:, None] == target[None, :, 0]) | (places[:, None] == target[None, :, 1])).astype(BF16)
    place_t = ((places[None, :] == target[:, :1]) | (places[None, :] == target[:, 1:])).astype(BF16)
    slot = jnp.arange(slots, dtype=jnp.int32)
    spread = slot // capacity * padded + slot % capacity
    pack = (spread[:, None] == places[None, :]).astype(BF16)
    unpack = (places[:, None] == spread[None, :]).astype(BF16)

    vmem = pl.BlockSpec(memory_space=pltpu.VMEM)
    dma = pltpu.SemaphoreType.DMA
    hidden, wgrad, tgrad = pl.pallas_call(
        functools.partial(kernel, (n_z, n_ctx, n_lo)),
        out_shape=(
            jax.ShapeDtypeStruct((slots, ff), BF16),
            jax.ShapeDtypeStruct((half, ff), BF16),
            jax.ShapeDtypeStruct((count, feat), BF16),
        ),
        in_specs=[vmem] * 5 + [pl.BlockSpec(memory_space=pl.ANY), vmem],
        out_specs=(vmem, vmem, vmem),
        scratch_shapes=[
            pltpu.VMEM(weights.shape[1:], BF16),
            pltpu.VMEM((n_ctx, padded, feat), BF16),
            pltpu.VMEM((n_ctx, padded, feat), BF16),
            pltpu.VMEM((n_tp, slots, feat), BF16),
            pltpu.VMEM((n_z, slots, feat), BF16),
            pltpu.VMEM((PARTS, slots, cols), F32),
            pltpu.VMEM((PARTS, n_z, slots, cols), BF16),
            pltpu.VMEM((n_lo, slots, feat), BF16),
            pltpu.VMEM((n_lo, slots, feat), BF16),
            pltpu.VMEM((n_lo, slots, feat), BF16),
            pltpu.VMEM((n_lo, slots, feat), BF16),
            pltpu.VMEM((n_ctx, padded, feat), BF16),
            pltpu.VMEM((n_ctx, padded, feat), BF16),
            pltpu.VMEM((PARTS, half, cols), BF16),
            pltpu.VMEM((PARTS, feat, cols), F32),
            pltpu.VMEM((PARTS, half, cols), BF16),
            dma,
            dma((n_ctx - 1,)), dma((n_ctx - 1,)),
            dma((n_lo,)), dma((n_lo,)),
            dma((n_lo,)), dma((n_lo,)),
            dma((n_lo,)), dma((n_z - 1,)), dma((n_z,)),
            dma((2, PARTS, n_z // 2)), dma((2, PARTS, n_z // 2)),
            dma((n_lo,)), dma((n_lo,)),
            dma((n_lo,)), dma((n_lo,)),
            dma((n_ctx - 1,)), dma((n_ctx - 1,)),
            dma((PARTS,)), dma((PARTS,)),
        ],
        compiler_params=pltpu.CompilerParams(
            collective_id=0, has_side_effects=True, vmem_limit_bytes=48 * 1024 * 1024
        ),
    )(tokens, place, place_t, pack, unpack, weights[0], cotangent[0, 0])
    return hidden[None, None], wgrad[None], tgrad


def solution(mesh):
    placed = (
        P(("dp", "ctx"), "tp"),
        P(("dp", "ctx"), None),
        P("ctx", None, "tp"),
        P("dp", "ctx", None, "tp"),
    )
    return jax.shard_map(
        per_device,
        mesh=mesh,
        in_specs=placed,
        out_specs=(P("dp", "ctx", None, "tp"), P("ctx", "dp", "tp"), P(("dp", "ctx"), "tp")),
        check_vma=False,
    )
```

time: 404 us -> 94 us (0.23)
  the two profiles are of different devices: /device:TPU:1 before, /device:TPU:48 now
where the time goes in v1:
time: 94 us; the launch traced here: 93.8 us
  Pallas kernels  86.7 us (92%)
  local copies, waits for them, and re-layouts  4.96 us (5%)
  other arithmetic  1.37 us (1%)
    pallas_call x1, Pallas kernels, per_device(): pl.pallas_call(functools.partial(kernel, (n_z, n_ctx, n_lo)), out_shape=(...  86.7 us
    unnamed x8, local copies, waits for them, and re-layouts  4.61 us

profile of v1, /device:TPU:48, one launch (start us, length us, event | category | flops | bytes accessed | tf_op | source)
XLA Modules:
  0.0 93.8 jit_solution(507988419894793706)
XLA Ops:
  0.6 0.8 copy.13
  1.4 0.1 eq.100
  1.6 0.1 fusion.4
  1.7 0.2 reduce_window_sum.11
  1.8 0.2 select_reduce_fusion
  2.0 0.1 reduce_sum.12
  2.1 0.1 copy.14
  2.2 0.7 multiply_add_fusion
  2.9 0.1 fusion.6.place_t
  3.1 0.1 fusion.1.pack
  3.2 0.0 copy-start
  3.2 1.0 %copy-done = bf16[1,1,144,1024]{3,2,1,0:T(8,128)(2,1)S(1)} copy-done((bf16[1,1,144,1024]{3,2,1,0:T(8,128)(2,1)S(1)}, bf16[1,1,144,1024]{3,2,1,0:T(8,128)(2,1)}, u32[]{:S(2)}) %copy-start) | copy-done | bytes 294936
  4.1 0.0 copy-start.1
  4.2 0.8 copy-done.1
  4.9 86.7 %shard_map.67 = (bf16[144,1024]{1,0:T(8,128)(2,1)S(1)}, bf16[192,1024]{1,0:T(8,128)(2,1)S(1)}, bf16[64,384]{1,0:T(8,128)(2,1)S(1)}) custom-call(bf16[64,384]{1,0:T(8,128)(2,1)S(1)} %copy-done.1, bf16[256,64]{1,0:T(8,128)(2,1)S(1)} %fusion.3.place, bf16[64,256]{1,0:T(8,128)(2,1)S(1)} %fusion.6.place_t, bf16[144,256]{1,0:T(8,128)(2,1)S(1)} %fusion.1.pack, ...), custom_call_target="tpu_custom_call" | custom-call | tf_op jit(solution)/shard_map/pallas_call | solution.py:280
  91.7 0.7 copy.18
  92.4 0.7 copy.19
  93.1 0.6 copy.20
  (4 shorter events, 0.1 us)
Async XLA Ops:
  3.2 1.0 %copy-start = (bf16[1,1,144,1024]{3,2,1,0:T(8,128)(2,1)S(1)}, bf16[1,1,144,1024]{3,2,1,0:T(8,128)(2,1)}, u32[]{:S(2)}) copy-start(bf16[1,1,144,1024]{3,2,1,0:T(8,128)(2,1)} %param.7) | copy-start | bytes 884740
  4.1 0.8 copy-start.1

commit v2 on v1

--- a/solution.py
+++ b/solution.py
@@ -12,6 +12,8 @@
 F32 = jnp.float32
 HI = 2
 CORES = 2
+ROWS = 16
+LANES = 128
 PARTS = 4
 
 
@@ -36,14 +38,15 @@
 
 def kernel(
     dims,
-    tokens, place, place_t, pack, unpack, w_hbm, cot,
-    hidden, wgrad, tgrad,
-    w, ysend, yrecv, g, r, acc, s, psend, precv, qsend, t, hsend, hrecv, wsend, wkeep, wrecv,
-    w_sem, y_ss, y_rs, gd_ss, gd_rs, gf_ss, gf_rs, r_ss, rf_ss, r_rs, s_ss, s_rs,
+    tokens_hbm, ids_hbm, w_hbm, cot_hbm,
+    hidden_hbm, wgrad_hbm, tgrad_hbm,
+    hidden, wgrad, tgrad, tokens, ids, cot, place, rt, w, ysend, yrecv, g, r, acc, s, psend, precv, qsend, t, hsend, hrecv, wsend, wkeep, wrecv,
+    in_sems, out_sems, y_ss, y_rs, gd_ss, gd_rs, gf_ss, gf_rs, r_ss, rf_ss, r_rs, s_ss, s_rs,
     p_ss, p_rs, t_ss, t_rs, h_ss, h_rs, x_ss, x_rs,
 ):
-    n_z, n_ctx, n_lo = dims
+    n_z, n_ctx, n_lo, capacity = dims
     feat = tokens.shape[1]
+    slots = cot.shape[0]
     cols = cot.shape[1] // PARTS
     half = feat // HI
     dp, e, j = lax.axis_index("dp"), lax.axis_index("ctx"), lax.axis_index("tp")
@@ -62,6 +65,13 @@
         made.start()
         waits.append(made)
 
+    stores = []
+
+    def store(src, dst):
+        made = pltpu.make_async_copy(src, dst, out_sems.at[len(stores)])
+        made.start()
+        stores.append(made)
+
     def on_y(d):
         return (dp, (e + d) % n_ctx, j)
 
@@ -74,8 +84,12 @@
     other = (dp, e, lo * CORES + 1 - core)
     across = (z * HI + 1 - hi, e, j)
 
-    w_copy = pltpu.make_async_copy(w_hbm, w, w_sem)
-    w_copy.start()
+    loads = [
+        pltpu.make_async_copy(src, dst, in_sems.at[i])
+        for i, (src, dst) in enumerate(((ids_hbm, ids), (tokens_hbm, tokens), (cot_hbm, cot), (w_hbm, w)))
+    ]
+    for load in loads:
+        load.start()
 
     partners = [on_y(d) for d in range(1, n_ctx)]
     partners += [on_z((z + d) % n_z) for d in range(1, n_z)]
@@ -85,20 +99,76 @@
     for to in partners:
         pl.semaphore_signal(barrier, inc=1, device_id=to, device_id_type=MESH)
 
-    ysend[...] = nn(place[...], tokens[...]).astype(BF16).reshape(ysend.shape)
+    count, folds = tokens.shape[0], feat // LANES
+    beyond = (capacity - ROWS) * folds
+    loads[0].wait()
+    name = lax.broadcasted_iota(jnp.int32, (n_ctx, count), 0)
+    named = ((ids[0:1, :] == name) | (ids[1:2, :] == name)).astype(F32)
+    earlier = lax.broadcasted_iota(jnp.int32, (count, count), 0) < lax.broadcasted_iota(jnp.int32, (count, count), 1)
+    rank = jnp.where(named > 0.0, nn(named.astype(BF16), earlier.astype(F32).astype(BF16)), -1.0)
+
+    def slot_of(row, kind):
+        if kind == 0:
+            return row
+        slot = jnp.full_like(row, -2)
+        for r in range(kind - 1, beyond, folds):
+            slot = jnp.where(row == r, ROWS + r // folds, slot)
+        return slot
+
+    row = lax.broadcasted_iota(jnp.int32, (ROWS, count), 0)
+    for kind in range(folds + 1):
+        slot = slot_of(row, kind).astype(F32)
+        for x in range(n_ctx):
+            place[kind, x * ROWS:(x + 1) * ROWS, :] = (rank[x:x + 1, :] == slot).astype(F32).astype(BF16)
+
+    def fold(mats, rows):
+        wide = nn(mats[0], rows)
+        tail = nn(mats[1], rows[:, 0:LANES])
+        for f in range(1, folds):
+            tail = tail + nn(mats[f + 1], rows[:, f * LANES:(f + 1) * LANES])
+        return jnp.concatenate([wide, tail], axis=1).astype(BF16).reshape(ysend.shape)
+
+    def unfold(mats, blocks, dot):
+        wide = dot(mats[0], blocks[:, 0:feat])
+        tail = blocks[:, feat:]
+        return wide + jnp.concatenate([dot(mats[f + 1], tail) for f in range(folds)], axis=1)
+
+    loads[1].wait()
+    ysend[...] = fold(place, tokens[...])
     pl.semaphore_wait(barrier, len(partners))
+
+    def spread(kind, rows_at):
+        shape = [slots, n_ctx * ROWS] if rows_at == 0 else [n_ctx * ROWS, slots]
+        want, col = lax.broadcasted_iota(jnp.int32, shape, rows_at), lax.broadcasted_iota(jnp.int32, shape, 1 - rows_at)
+        within = slot_of(col & (ROWS - 1), kind)
+        same = ((col >> (ROWS.bit_length() - 1)) * capacity + within == want) & (within >= 0)
+        return same.astype(F32).astype(BF16)
 
     far = sorted(range(1, n_ctx), key=lambda d: -min(d, n_ctx - d))
     for d in far:
         send(ysend.at[(e + d) % n_ctx], yrecv.at[e], y_ss.at[d - 1], y_rs.at[d - 1], on_y(d))
     yrecv[e] = ysend[e]
+    pack = [spread(kind, 0) for kind in range(folds + 1)]
     for d in far:
         copy(ysend.at[0], yrecv.at[(e - d + n_ctx) % n_ctx], y_ss.at[d - 1], y_rs.at[d - 1], on_y(d)).wait_recv()
-    g[j] = nn(pack[...], yrecv[...].reshape(-1, feat)).astype(BF16)
-
-    for o in range(1, n_lo):
+    g[j] = unfold(pack, yrecv[...].reshape(-1, feat + LANES), nn).astype(BF16)
+
+    near = [o for o in (2, 1) if o < n_lo]
+    inner = (lo + 1) // 2 % 2 == 1
+    end = 3
+    direct = copy(g.at[j], g.at[j], gd_ss.at[n_lo - 1], gd_rs.at[n_lo - 1], on_lo(n_lo - 1))
+    passed = xor(lo, n_lo // 2) * CORES + core
+    through = copy(g.at[passed], g.at[passed], gd_ss.at[0], gd_rs.at[n_lo - 1], on_lo(1))
+    send(g.at[j], g.at[j], gd_ss.at[near[0]], gd_rs.at[near[0]], on_lo(near[0]))
+    if n_lo > end:
+
+        @pl.when(inner)
+        def _():
+            direct.start()
+
+    send(g.at[j], g.at[j], gf_ss.at[0], gf_rs.at[0], other)
+    for o in near[1:]:
         send(g.at[j], g.at[j], gd_ss.at[o], gd_rs.at[o], on_lo(o))
-    send(g.at[j], g.at[j], gf_ss.at[0], gf_rs.at[0], other)
 
     def rows_copy(o):
         k = xor(lo, o) * CORES + core
@@ -119,21 +189,30 @@
             acc[q] = term if first else acc[q] + term
 
     rows_start(0)
-    w_copy.wait()
+    loads[3].wait()
     project(j, True)
     k = lo * CORES + 1 - core
     copy(g.at[j], g.at[k], gf_ss.at[0], gf_rs.at[0], other).wait_recv()
     project(k)
-    for o in range(1, n_lo):
+    order = near + [end] * (n_lo > end)
+    for o in order:
         k = xor(lo, o) * CORES + core
         copy(g.at[j], g.at[k], gd_ss.at[o], gd_rs.at[o], on_lo(o)).wait_recv()
+        if n_lo > end and o == near[0]:
+
+            @pl.when(inner)
+            def _():
+                through.start()
+
         send(g.at[k], g.at[k], gf_ss.at[o], gf_rs.at[o], other)
         rows_start(o)
         project(k)
-    for o in range(1, n_lo):
+    for o in order:
         k = xor(lo, o) * CORES + 1 - core
         copy(g.at[j], g.at[k], gf_ss.at[o], gf_rs.at[o], other).wait_recv()
-        project(k)
+        if o != order[-1]:
+            project(k)
+    last = k
 
     def reach(way, q):
         return n_z // 2 if q % 2 == way else n_z - 1 - n_z // 2
@@ -153,14 +232,14 @@
                 if d < reach(way, q):
                     send(s.at[q, src], s.at[q, src], s_ss.at[way, q, d], s_rs.at[way, q, d], step_to(way))
 
+    loads[2].wait()
     for q in range(PARTS):
         at = slice(q * cols, (q + 1) * cols)
-        p = acc[q]
+        p = acc[q] + nn(g[last], w[pl.ds(pl.multiple_of(last * feat, feat), feat), at])
+        acc[q] = p
         gate = jax.nn.sigmoid(p)
-        hidden[:, at] = (p * gate).astype(BF16)
         s[q, z] = (cot[:, at].astype(F32) * gate * (1.0 + p * (1.0 - gate))).astype(BF16)
-        if q < 2:
-            own(q)
+        own(q)
 
     def back(k):
         rows = pl.ds(pl.multiple_of(k * feat, feat), feat)
@@ -173,8 +252,14 @@
         psend[m] = back(m * CORES + 1 - core).astype(BF16)
         send(psend.at[m], precv.at[m], p_ss.at[m], p_rs.at[m], other)
 
-    for d in (1,):
-        step(0, d), step(1, d)
+    first, second = (0, 1), (2, 3)
+    n_d = n_z // 2
+
+    def steps(part, d):
+        for q in part:
+            step(q, d)
+
+    steps(first, 1)
 
     for m in range(n_lo):
         copy(psend.at[m], precv.at[m], p_ss.at[m], p_rs.at[m], other).wait_recv()
@@ -184,12 +269,9 @@
         if o:
             send(qsend.at[o], t.at[o], t_ss.at[o], t_rs.at[o], on_lo(o))
 
-    for d in range(2, n_z // 2):
-        step(0, d), step(1, d)
-        if d == 2:
-            own(2), own(3)
-    if n_z // 2 <= 2:
-        own(2), own(3)
+    if n_d > 2:
+        steps(first, 2)
+    steps(second, 1)
 
     r[z] = g[z]
     for d in range(1, n_z):
@@ -200,46 +282,67 @@
         def _():
             copy(r.at[src], r.at[src], rf_ss.at[d - 1], r_rs.at[src], other).start()
 
-    step(0, n_z // 2), step(1, n_z // 2)
-    step(2, 1), step(3, 1)
-
-    def product(q):
-        right = s[q].reshape(-1, cols)
-        whole = tn(r[...].reshape(-1, feat), right)
-        wkeep[q] = whole
-        theirs = wkeep[q, pl.ds(pl.multiple_of((1 - hi) * half, half), half), :]
-        wsend[q] = theirs.astype(BF16)
+    for d in range(3, n_d):
+        steps(first, d)
+        steps(second, d - 1)
+
+    rt[...] = r[...].reshape(-1, feat).T
+    for q in range(PARTS):
+        p = acc[q]
+        hidden[:, q * cols:(q + 1) * cols] = (p * jax.nn.sigmoid(p)).astype(BF16)
+    store(hidden, hidden_hbm)
+
+    def product(q, side):
+        return nn(rt[pl.ds(pl.multiple_of(side * half, half), half), :], s[q].reshape(-1, cols))
+
+    def theirs(q):
+        wsend[q] = product(q, 1 - hi).astype(BF16)
         send(wsend.at[q], wrecv.at[q], x_ss.at[q], x_rs.at[q], across)
 
-    product(0)
-    product(1)
-    step(2, 2), step(3, 2)
+    steps(first, n_d)
+    for q in first:
+        theirs(q)
+    if n_d > 2:
+        steps(second, n_d - 1)
 
     summed = qsend[0].astype(F32)
     for o in range(1, n_lo):
         copy(qsend.at[o], t.at[o], t_ss.at[o], t_rs.at[o], on_lo(o)).wait_recv()
         summed = summed + t[o].astype(F32)
-    hsend[...] = nn(unpack[...], summed.astype(BF16)).astype(BF16).reshape(hsend.shape)
+    hsend[...] = fold([spread(kind, 1) for kind in range(folds + 1)], summed.astype(BF16))
     for d in far:
         send(hsend.at[(e + d) % n_ctx], hrecv.at[e], h_ss.at[d - 1], h_rs.at[d - 1], on_y(d))
     hrecv[e] = hsend[e]
 
-    for d in range(3, n_z // 2 + 1):
-        step(2, d), step(3, d)
-    product(2)
-    product(3)
+    for q in first:
+        wkeep[q] = product(q, hi)
+    steps(second, n_d)
+    for q in second:
+        theirs(q)
+    for q in second:
+        wkeep[q] = product(q, hi)
 
     for d in far:
         copy(hsend.at[0], hrecv.at[(e - d + n_ctx) % n_ctx], h_ss.at[d - 1], h_rs.at[d - 1], on_y(d)).wait_recv()
-    tgrad[...] = nn(place_t[...], hrecv[...].reshape(-1, feat)).astype(BF16)
+    tgrad[...] = unfold(place, hrecv[...].reshape(-1, feat + LANES), tn).astype(BF16)
+    store(tgrad, tgrad_hbm)
 
     for q in range(PARTS):
         copy(wsend.at[q], wrecv.at[q], x_ss.at[q], x_rs.at[q], across).wait_recv()
-        mine = wkeep[q, pl.ds(pl.multiple_of(hi * half, half), half), :]
-        wgrad[:, q * cols:(q + 1) * cols] = (mine + wrecv[q].astype(F32)).astype(BF16)
+        at = slice(q * cols, (q + 1) * cols)
+        wgrad[:, at] = (wkeep[q] + wrecv[q].astype(F32)).astype(BF16)
+        store(wgrad.at[:, at], wgrad_hbm.at[:, at])
 
     for made in waits:
         made.wait_send()
+    for made in stores:
+        made.wait()
+    if n_lo > end:
+
+        @pl.when(inner)
+        def _():
+            direct.wait_send()
+            through.wait_send()
     for o in range(n_lo):
         k, made = rows_copy(o)
 
@@ -260,36 +363,30 @@
     count, feat = tokens.shape
     slots, ff = cotangent.shape[2:]
     capacity = slots // n_ctx
-    padded = -(-capacity // 16) * 16
     cols, half = ff // PARTS, feat // HI
 
-    routed = expert_ids.reshape(-1)
-    onehot = (routed[:, None] == jnp.arange(n_ctx, dtype=jnp.int32)[None, :]).astype(jnp.int32)
-    before = jnp.cumsum(onehot, axis=0) - onehot
-    target = (routed * padded + jnp.sum(before * onehot, axis=1)).reshape(count, 2)
-    places = jnp.arange(n_ctx * padded, dtype=jnp.int32)
-    place = ((places[:, None] == target[None, :, 0]) | (places[:, None] == target[None, :, 1])).astype(BF16)
-    place_t = ((places[None, :] == target[:, :1]) | (places[None, :] == target[:, 1:])).astype(BF16)
-    slot = jnp.arange(slots, dtype=jnp.int32)
-    spread = slot // capacity * padded + slot % capacity
-    pack = (spread[:, None] == places[None, :]).astype(BF16)
-    unpack = (places[:, None] == spread[None, :]).astype(BF16)
-
-    vmem = pl.BlockSpec(memory_space=pltpu.VMEM)
     dma = pltpu.SemaphoreType.DMA
     hidden, wgrad, tgrad = pl.pallas_call(
-        functools.partial(kernel, (n_z, n_ctx, n_lo)),
+        functools.partial(kernel, (n_z, n_ctx, n_lo, capacity)),
         out_shape=(
             jax.ShapeDtypeStruct((slots, ff), BF16),
             jax.ShapeDtypeStruct((half, ff), BF16),
             jax.ShapeDtypeStruct((count, feat), BF16),
         ),
-        in_specs=[vmem] * 5 + [pl.BlockSpec(memory_space=pl.ANY), vmem],
-        out_specs=(vmem, vmem, vmem),
+        in_specs=[pl.BlockSpec(memory_space=pl.ANY)] * 4,
+        out_specs=[pl.BlockSpec(memory_space=pl.ANY)] * 3,
         scratch_shapes=[
+            pltpu.VMEM((slots, ff), BF16),
+            pltpu.VMEM((half, ff), BF16),
+            pltpu.VMEM((count, feat), BF16),
+            pltpu.VMEM((count, feat), BF16),
+            pltpu.VMEM((2, count), jnp.int32),
+            pltpu.VMEM((slots, ff), BF16),
+            pltpu.VMEM((feat // LANES + 1, n_ctx * ROWS, count), BF16),
+            pltpu.VMEM((feat, n_z * slots), BF16),
             pltpu.VMEM(weights.shape[1:], BF16),
-            pltpu.VMEM((n_ctx, padded, feat), BF16),
-            pltpu.VMEM((n_ctx, padded, feat), BF16),
+            pltpu.VMEM((n_ctx, ROWS, feat + LANES), BF16),
+            pltpu.VMEM((n_ctx, ROWS, feat + LANES), BF16),
             pltpu.VMEM((n_tp, slots, feat), BF16),
             pltpu.VMEM((n_z, slots, feat), BF16),
             pltpu.VMEM((PARTS, slots, cols), F32),
@@ -298,12 +395,12 @@
             pltpu.VMEM((n_lo, slots, feat), BF16),
             pltpu.VMEM((n_lo, slots, feat), BF16),
             pltpu.VMEM((n_lo, slots, feat), BF16),
-            pltpu.VMEM((n_ctx, padded, feat), BF16),
-            pltpu.VMEM((n_ctx, padded, feat), BF16),
+            pltpu.VMEM((n_ctx, ROWS, feat + LANES), BF16),
+            pltpu.VMEM((n_ctx, ROWS, feat + LANES), BF16),
             pltpu.VMEM((PARTS, half, cols), BF16),
-            pltpu.VMEM((PARTS, feat, cols), F32),
+            pltpu.VMEM((PARTS, half, cols), F32),
             pltpu.VMEM((PARTS, half, cols), BF16),
-            dma,
+            dma((4,)), dma((2 + PARTS,)),
             dma((n_ctx - 1,)), dma((n_ctx - 1,)),
             dma((n_lo,)), dma((n_lo,)),
             dma((n_lo,)), dma((n_lo,)),
@@ -317,7 +414,7 @@
         compiler_params=pltpu.CompilerParams(
             collective_id=0, has_side_effects=True, vmem_limit_bytes=48 * 1024 * 1024
         ),
-    )(tokens, place, place_t, pack, unpack, weights[0], cotangent[0, 0])
+    )(tokens, expert_ids.T, weights[0], cotangent[0, 0])
     return hidden[None, None], wgrad[None], tgrad
 
 

time: 94 us -> 88.3 us (0.939)
  the two profiles are of different devices: /device:TPU:48 before, /device:TPU:1 now
where the time goes in v2:
time: 88.3 us; the launch traced here: 88 us
  Pallas kernels  82.9 us (94%)
  local copies, waits for them, and re-layouts  4.51 us (5%)
    pallas_call x1, Pallas kernels, per_device(): pl.pallas_call(functools.partial(kernel, (n_z, n_ctx, n_lo, capacity)), o...  82.9 us
    unnamed x9, local copies, waits for them, and re-layouts  4.51 us

profile of v2, /device:TPU:1, one launch (start us, length us, event | category | flops | bytes accessed | tf_op | source)
XLA Modules:
  0.0 88.0 jit_solution(1853857346851029982)
XLA Ops:
  0.6 0.0 copy-start
  0.6 1.0 %copy-done = bf16[1,1,144,1024]{3,2,1,0:T(8,128)(2,1)S(1)} copy-done((bf16[1,1,144,1024]{3,2,1,0:T(8,128)(2,1)S(1)}, bf16[1,1,144,1024]{3,2,1,0:T(8,128)(2,1)}, u32[]{:S(2)}) %copy-start) | copy-done | bytes 294936
  1.6 0.0 copy-start.1
  1.6 0.8 copy-done.1
  2.4 0.0 copy-start.2
  2.4 0.7 copy-done.2
  3.1 82.9 %shard_map.67 = (bf16[144,1024]{1,0:T(8,128)(2,1)S(1)}, bf16[192,1024]{1,0:T(8,128)(2,1)S(1)}, bf16[64,384]{1,0:T(8,128)(2,1)S(1)}) custom-call(bf16[64,384]{1,0:T(8,128)(2,1)S(1)} %copy-done.1, s32[2,64]{1,0:T(2,128)S(1)} %bitcast.8, bf16[3072,1024]{1,0:T(8,128)(2,1)} %bitcast.9, bf16[144,1024]{1,0:T(8,128)(2,1)S(1)} %bitcast.6), custom_call_target="tpu_custom_call" | custom-call | tf_op jit(solution)/shard_map/pallas_call | solution.py:369
  86.0 0.7 copy.10
  86.7 0.7 copy.11
  87.4 0.6 copy.12
Async XLA Ops:
  0.6 1.0 %copy-start = (bf16[1,1,144,1024]{3,2,1,0:T(8,128)(2,1)S(1)}, bf16[1,1,144,1024]{3,2,1,0:T(8,128)(2,1)}, u32[]{:S(2)}) copy-start(bf16[1,1,144,1024]{3,2,1,0:T(8,128)(2,1)} %param.7) | copy-start | bytes 884740
  1.6 0.8 copy-start.1
  2.4 0.7 copy-start.2

commit v3 on v2

--- a/solution.py
+++ b/solution.py
@@ -170,6 +170,9 @@
     for o in near[1:]:
         send(g.at[j], g.at[j], gd_ss.at[o], gd_rs.at[o], on_lo(o))
 
+    row_sender = (core + z + lo) % 2 == 0
+    row_taker = core == z % CORES
+
     def rows_copy(o):
         k = xor(lo, o) * CORES + core
         return k, copy(g.at[k], r.at[z], r_ss.at[o], r_rs.at[z], on_z(k))
@@ -177,7 +180,7 @@
     def rows_start(o):
         k, made = rows_copy(o)
 
-        @pl.when(k != z)
+        @pl.when((k != z) & row_sender)
         def _():
             made.start()
 
@@ -259,6 +262,27 @@
         for q in part:
             step(q, d)
 
+    r[z] = g[z]
+
+    def rows_in(d):
+        src = (z + d) % n_z
+        copy(g.at[0], r.at[src], r_ss.at[0], r_rs.at[src], other).wait_recv()
+
+    def rows_on(d):
+        src = (z + d) % n_z
+        return (
+            copy(r.at[src], r.at[src], rf_ss.at[0, d - 1], r_rs.at[src], other),
+            copy(r.at[src], r.at[src], rf_ss.at[1, d - 1], r_rs.at[src], on_lo(1)),
+        )
+
+    for d in range(1, n_z):
+
+        @pl.when(row_taker & (lo % 2 == d % 2))
+        def _():
+            rows_in(d)
+            for made in rows_on(d):
+                made.start()
+
     steps(first, 1)
 
     for m in range(n_lo):
@@ -273,14 +297,16 @@
         steps(first, 2)
     steps(second, 1)
 
-    r[z] = g[z]
     for d in range(1, n_z):
-        src = (z + d) % n_z
-        copy(g.at[0], r.at[src], rf_ss.at[d - 1], r_rs.at[src], other).wait_recv()
-
-        @pl.when(core == z % CORES)
-        def _():
-            copy(r.at[src], r.at[src], rf_ss.at[d - 1], r_rs.at[src], other).start()
+
+        @pl.when(row_taker & (lo % 2 != d % 2))
+        def _():
+            rows_in(d)
+            rows_on(d)[0].start()
+
+        @pl.when(jnp.logical_not(row_taker))
+        def _():
+            rows_in(d)
 
     for d in range(3, n_d):
         steps(first, d)
@@ -346,15 +372,19 @@
     for o in range(n_lo):
         k, made = rows_copy(o)
 
-        @pl.when(k != z)
+        @pl.when((k != z) & row_sender)
         def _():
             made.wait_send()
 
-    @pl.when(core == z % CORES)
-    def _():
-        for d in range(1, n_z):
-            src = (z + d) % n_z
-            copy(r.at[src], r.at[src], rf_ss.at[d - 1], r_rs.at[src], other).wait_send()
+    for d in range(1, n_z):
+
+        @pl.when(row_taker)
+        def _():
+            rows_on(d)[0].wait_send()
+
+        @pl.when(row_taker & (lo % 2 == d % 2))
+        def _():
+            rows_on(d)[1].wait_send()
 
 
 def per_device(tokens, expert_ids, weights, cotangent):
@@ -404,7 +434,7 @@
             dma((n_ctx - 1,)), dma((n_ctx - 1,)),
             dma((n_lo,)), dma((n_lo,)),
             dma((n_lo,)), dma((n_lo,)),
-            dma((n_lo,)), dma((n_z - 1,)), dma((n_z,)),
+            dma((n_lo,)), dma((2, n_z - 1)), dma((n_z,)),
             dma((2, PARTS, n_z // 2)), dma((2, PARTS, n_z // 2)),
             dma((n_lo,)), dma((n_lo,)),
             dma((n_lo,)), dma((n_lo,)),

time: 88.3 us -> 85.7 us (0.971)
  Pallas kernels: 82.9 us -> 80.2 us
    pallas_call x1, Pallas kernels: 82.9 us -> 80.2 us  [per_device(): pl.pallas_call(functools.partial(kernel, (n_z, n_ctx, n_lo, capacity)), o...]
where the time goes in v3:
time: 85.7 us; the launch traced here: 85.4 us
  Pallas kernels  80.2 us (94%)
  local copies, waits for them, and re-layouts  4.51 us (5%)
    pallas_call x1, Pallas kernels, per_device(): pl.pallas_call(functools.partial(kernel, (n_z, n_ctx, n_lo, capacity)), o...  80.2 us
    unnamed x9, local copies, waits for them, and re-layouts  4.51 us

profile of v3, /device:TPU:1, one launch (start us, length us, event | category | flops | bytes accessed | tf_op | source)
XLA Modules:
  0.0 85.4 jit_solution(16948314848050172786)
XLA Ops:
  0.6 0.0 copy-start
  0.6 1.0 %copy-done = bf16[1,1,144,1024]{3,2,1,0:T(8,128)(2,1)S(1)} copy-done((bf16[1,1,144,1024]{3,2,1,0:T(8,128)(2,1)S(1)}, bf16[1,1,144,1024]{3,2,1,0:T(8,128)(2,1)}, u32[]{:S(2)}) %copy-start) | copy-done | bytes 294936
  1.6 0.0 copy-start.1
  1.6 0.8 copy-done.1
  2.4 0.0 copy-start.2
  2.4 0.7 copy-done.2
  3.1 80.2 %shard_map.67 = (bf16[144,1024]{1,0:T(8,128)(2,1)S(1)}, bf16[192,1024]{1,0:T(8,128)(2,1)S(1)}, bf16[64,384]{1,0:T(8,128)(2,1)S(1)}) custom-call(bf16[64,384]{1,0:T(8,128)(2,1)S(1)} %copy-done.1, s32[2,64]{1,0:T(2,128)S(1)} %bitcast.8, bf16[3072,1024]{1,0:T(8,128)(2,1)} %bitcast.9, bf16[144,1024]{1,0:T(8,128)(2,1)S(1)} %bitcast.6), custom_call_target="tpu_custom_call" | custom-call | tf_op jit(solution)/shard_map/pallas_call | solution.py:399
  83.3 0.7 copy.10
  84.0 0.7 copy.11
  84.8 0.6 copy.12
Async XLA Ops:
  0.6 1.0 %copy-start = (bf16[1,1,144,1024]{3,2,1,0:T(8,128)(2,1)S(1)}, bf16[1,1,144,1024]{3,2,1,0:T(8,128)(2,1)}, u32[]{:S(2)}) copy-start(bf16[1,1,144,1024]{3,2,1,0:T(8,128)(2,1)} %param.7) | copy-start | bytes 884740
  1.6 0.8 copy-start.1
  2.4 0.7 copy-start.2

commit v4 on v3

--- a/solution.py
+++ b/solution.py
@@ -38,17 +38,20 @@
 
 def kernel(
     dims,
-    tokens_hbm, ids_hbm, w_hbm, cot_hbm,
-    hidden_hbm, wgrad_hbm, tgrad_hbm,
+    small, w_hbm,
+    wide_out,
     hidden, wgrad, tgrad, tokens, ids, cot, place, rt, w, ysend, yrecv, g, r, acc, s, psend, precv, qsend, t, hsend, hrecv, wsend, wkeep, wrecv,
     in_sems, out_sems, y_ss, y_rs, gd_ss, gd_rs, gf_ss, gf_rs, r_ss, rf_ss, r_rs, s_ss, s_rs,
     p_ss, p_rs, t_ss, t_rs, h_ss, h_rs, x_ss, x_rs,
 ):
     n_z, n_ctx, n_lo, capacity = dims
-    feat = tokens.shape[1]
-    slots = cot.shape[0]
+    slots, count, feat = cot.shape[0], tokens.shape[0], tokens.shape[1]
+    cot_hbm, tokens_hbm = small.at[0:slots], small.at[slots:slots + count, 0:feat]
+    ids_hbm = small.at[slots + count:, 0:ids.shape[1]]
+    half = feat // HI
+    hidden_hbm, wgrad_hbm = wide_out.at[0:slots], wide_out.at[slots:slots + half]
+    tgrad_hbm = wide_out.at[slots + half:, 0:feat]
     cols = cot.shape[1] // PARTS
-    half = feat // HI
     dp, e, j = lax.axis_index("dp"), lax.axis_index("ctx"), lax.axis_index("tp")
     z, hi = dp // HI, dp % HI
     lo, core = j // CORES, j % CORES
@@ -99,11 +102,11 @@
     for to in partners:
         pl.semaphore_signal(barrier, inc=1, device_id=to, device_id_type=MESH)
 
-    count, folds = tokens.shape[0], feat // LANES
+    folds = feat // LANES
     beyond = (capacity - ROWS) * folds
     loads[0].wait()
-    name = lax.broadcasted_iota(jnp.int32, (n_ctx, count), 0)
-    named = ((ids[0:1, :] == name) | (ids[1:2, :] == name)).astype(F32)
+    name = lax.broadcasted_iota(jnp.int32, (n_ctx, count), 0).astype(F32)
+    named = ((ids[0:1, 0:count].astype(F32) == name) | (ids[1:2, 0:count].astype(F32) == name)).astype(F32)
     earlier = lax.broadcasted_iota(jnp.int32, (count, count), 0) < lax.broadcasted_iota(jnp.int32, (count, count), 1)
     rank = jnp.where(named > 0.0, nn(named.astype(BF16), earlier.astype(F32).astype(BF16)), -1.0)
 
@@ -325,8 +328,8 @@
         wsend[q] = product(q, 1 - hi).astype(BF16)
         send(wsend.at[q], wrecv.at[q], x_ss.at[q], x_rs.at[q], across)
 
-    steps(first, n_d)
     for q in first:
+        step(q, n_d)
         theirs(q)
     if n_d > 2:
         steps(second, n_d - 1)
@@ -342,8 +345,8 @@
 
     for q in first:
         wkeep[q] = product(q, hi)
-    steps(second, n_d)
     for q in second:
+        step(q, n_d)
         theirs(q)
     for q in second:
         wkeep[q] = product(q, hi)
@@ -396,21 +399,21 @@
     cols, half = ff // PARTS, feat // HI
 
     dma = pltpu.SemaphoreType.DMA
-    hidden, wgrad, tgrad = pl.pallas_call(
+    def wide(rows, height):
+        return jnp.pad(rows, ((0, height - rows.shape[0]), (0, ff - rows.shape[1])))
+
+    small = jnp.concatenate([cotangent[0, 0], wide(tokens, count), wide(expert_ids.T.astype(BF16), 16)])
+    out = pl.pallas_call(
         functools.partial(kernel, (n_z, n_ctx, n_lo, capacity)),
-        out_shape=(
-            jax.ShapeDtypeStruct((slots, ff), BF16),
-            jax.ShapeDtypeStruct((half, ff), BF16),
-            jax.ShapeDtypeStruct((count, feat), BF16),
-        ),
-        in_specs=[pl.BlockSpec(memory_space=pl.ANY)] * 4,
-        out_specs=[pl.BlockSpec(memory_space=pl.ANY)] * 3,
+        out_shape=jax.ShapeDtypeStruct((slots + half + count, ff), BF16),
+        in_specs=[pl.BlockSpec(memory_space=pl.ANY)] * 2,
+        out_specs=pl.BlockSpec(memory_space=pl.ANY),
         scratch_shapes=[
             pltpu.VMEM((slots, ff), BF16),
             pltpu.VMEM((half, ff), BF16),
             pltpu.VMEM((count, feat), BF16),
             pltpu.VMEM((count, feat), BF16),
-            pltpu.VMEM((2, count), jnp.int32),
+            pltpu.VMEM((16, LANES), BF16),
             pltpu.VMEM((slots, ff), BF16),
             pltpu.VMEM((feat // LANES + 1, n_ctx * ROWS, count), BF16),
             pltpu.VMEM((feat, n_z * slots), BF16),
@@ -444,8 +447,8 @@
         compiler_params=pltpu.CompilerParams(
             collective_id=0, has_side_effects=True, vmem_limit_bytes=48 * 1024 * 1024
         ),
-    )(tokens, expert_ids.T, weights[0], cotangent[0, 0])
-    return hidden[None, None], wgrad[None], tgrad
+    )(small, weights[0])
+    return out[None, None, :slots], out[None, slots:slots + half], out[slots + half:, :feat]
 
 
 def solution(mesh):

time: 85.7 us -> 84.5 us (0.986)
  local copies, waits for them, and re-layouts: 4.51 us -> 2.13 us
  other arithmetic: 0 us -> 1.72 us
    unnamed x9 -> x0, local copies, waits for them, and re-layouts: 4.51 us -> none
    broadcast_in_dim x0 -> x2, local copies, waits for them, and re-layouts: none -> 1.5 us  [the longest x1 0.77 us: per_device(): out[None, slots:slots + half]]
    concatenate x0 -> x1, other arithmetic: none -> 1.03 us  [per_device(): jnp.concatenate([cotangent[0, 0], wide(tokens, count), wide(expert_ids.T....]
where the time goes in v4:
time: 84.5 us; the launch traced here: 84.4 us
  Pallas kernels  79.9 us (95%)
  local copies, waits for them, and re-layouts  2.13 us (3%)
  other arithmetic  1.72 us (2%)
    pallas_call x1, Pallas kernels, per_device(): pl.pallas_call(functools.partial(kernel, (n_z, n_ctx, n_lo, capacity)), o...  79.9 us

profile of v4, /device:TPU:1, one launch (start us, length us, event | category | flops | bytes accessed | tf_op | source)
XLA Modules:
  0.0 84.4 jit_solution(550263945521854631)
XLA Ops:
  0.6 0.7 convert_bitcast_fusion
  1.3 1.0 %fusion.4.small = bf16[224,1024]{1,0:T(8,128)(2,1)S(1)} fusion(bf16[2,64]{1,0:T(2,128)(2,1)S(1)} %convert_bitcast_fusion, bf16[64,384]{1,0:T(8,128)(2,1)} %param.4, bf16[144,1024]{1,0:T(8,128)(2,1)} %bitcast.9), kind=kLoop, calls=%fused_computation.7 | loop fusion | flops 2752512 | bytes 803072 | tf_op jit(solution)/shard_map/concatenate | solution.py:405
  2.4 79.9 %shard_map.67 = bf16[400,1024]{1,0:T(8,128)(2,1)S(1)} custom-call(bf16[224,1024]{1,0:T(8,128)(2,1)S(1)} %fusion.4.small, bf16[3072,1024]{1,0:T(8,128)(2,1)} %bitcast.8), custom_call_target="tpu_custom_call" | custom-call | tf_op jit(solution)/shard_map/pallas_call | solution.py:406
  82.2 0.6 slice.11
  82.8 0.7 slice_bitcast_fusion.1
  83.6 0.8 slice_bitcast_fusion

commit v5 on v4

--- a/solution.py
+++ b/solution.py
@@ -245,7 +245,8 @@
         acc[q] = p
         gate = jax.nn.sigmoid(p)
         s[q, z] = (cot[:, at].astype(F32) * gate * (1.0 + p * (1.0 - gate))).astype(BF16)
-        own(q)
+        if q < PARTS - 1:
+            own(q)
 
     def back(k):
         rows = pl.ds(pl.multiple_of(k * feat, feat), feat)
@@ -287,6 +288,7 @@
                 made.start()
 
     steps(first, 1)
+    own(PARTS - 1)
 
     for m in range(n_lo):
         copy(psend.at[m], precv.at[m], p_ss.at[m], p_rs.at[m], other).wait_recv()

time: 84.5 us -> 84.1 us (level)
  Pallas kernels: 79.9 us -> 79 us
    pallas_call x1, Pallas kernels: 79.9 us -> 79 us  [per_device(): pl.pallas_call(functools.partial(kernel, (n_z, n_ctx, n_lo, capacity)), o...]
where the time goes in v5:
time: 84.1 us; the launch traced here: 83.5 us
  Pallas kernels  79 us (94%)
  local copies, waits for them, and re-layouts  2.13 us (3%)
  other arithmetic  1.72 us (2%)
    pallas_call x1, Pallas kernels, per_device(): pl.pallas_call(functools.partial(kernel, (n_z, n_ctx, n_lo, capacity)), o...  79 us

profile of v5, /device:TPU:1, one launch (start us, length us, event | category | flops | bytes accessed | tf_op | source)
XLA Modules:
  0.0 83.5 jit_solution(12225521406528614714)
XLA Ops:
  0.6 0.7 convert_bitcast_fusion
  1.3 1.0 %fusion.4.small = bf16[224,1024]{1,0:T(8,128)(2,1)S(1)} fusion(bf16[2,64]{1,0:T(2,128)(2,1)S(1)} %convert_bitcast_fusion, bf16[64,384]{1,0:T(8,128)(2,1)} %param.4, bf16[144,1024]{1,0:T(8,128)(2,1)} %bitcast.9), kind=kLoop, calls=%fused_computation.7 | loop fusion | flops 2752512 | bytes 803072 | tf_op jit(solution)/shard_map/concatenate | solution.py:407
  2.4 79.0 %shard_map.67 = bf16[400,1024]{1,0:T(8,128)(2,1)S(1)} custom-call(bf16[224,1024]{1,0:T(8,128)(2,1)S(1)} %fusion.4.small, bf16[3072,1024]{1,0:T(8,128)(2,1)} %bitcast.8), custom_call_target="tpu_custom_call" | custom-call | tf_op jit(solution)/shard_map/pallas_call | solution.py:408
  81.4 0.6 slice.11
  82.0 0.7 slice_bitcast_fusion.1
  82.7 0.8 slice_bitcast_fusion
